TPU v7x, 512 devices: a whole 4x8x8 slice. The times are simulated.
512 devices in a mesh: section: 32 (over x, y), patch: 16 (over z, core).
Axes of the slice: x: 4, y: 8, z: 8, core: 2. Of those that a mesh axis runs over, the one named last changes fastest.
Arguments:
- previous: bfloat16 [32, 256, 2048], P('section', 'patch'), may hold values from -6 to 6
- stale_keys: bfloat16 [32, 2, 256, 2048], P('section'), may hold values from -12 to 12
- stale_values: bfloat16 [32, 2, 256, 2048], P('section'), may hold values from -6 to 6
- modulation: float32 [32, 2, 3, 2048], P('section'), may hold values from -4 to 4
- q_gain: float32 [32, 2, 128], P('section'), as said below
- k_gain: float32 [32, 2, 128], P('section'), as said below
- blocks: int32 [32], P('section'), may hold values from 1 to 2, as said below
- refresh: int32 [32, 16], P('section'), may hold values from 0 to 1, as said below
Outputs:
- mixed: float32 [32, 256, 2048], P('section', 'patch')
Inputs may be any that keep to these rules, and one draw needn't show every extreme that they name: Every section runs 1 to 2 blocks and some section runs 2. `refresh`: in every section exactly 4 patches have 1, the others 0. `q_gain`: real gains. `k_gain`: real gains.
All inputs are finite; a program needn't handle non-finite values.
Results may differ from a plain program's by a relative error of at most 0.008.
The roundings to bfloat16 on the way count: a program that leaves them out, or rounds other values in their place, can miss the bound.
Values may be sent and summed in bfloat16 or wider, within the bound.
A program may use at most 64 MiB of HBM per device.

v0:
```python
import math

import jax
import jax.numpy as jnp
from jax import lax
from jax.sharding import PartitionSpec as P

epsilon = 1e-06


def passed_along(block, axis, distance):
    devices = range(lax.axis_size(axis))
    route = [((i - distance) % len(devices), i) for i in devices]
    return lax.ppermute(block, axis, route)


def rms_scale(values_in):
    return values_in * lax.rsqrt(jnp.mean(values_in * values_in, axis=-1, keepdims=True) + epsilon)


def prepare(rows, modulate, q_scale, k_scale, head_count, head_size):
    tok_rows = rows.shape[0]
    modded = rms_scale(rows) * (1.0 + modulate[1]) + modulate[0]
    normed = rms_scale(modded.reshape(tok_rows, head_count, head_size))
    query = (normed * q_scale * (1.0 / math.sqrt(head_size))).astype(jnp.bfloat16)
    fresh_k = (normed * k_scale).astype(jnp.bfloat16).reshape(tok_rows, head_count * head_size)
    fresh_v = modded.astype(jnp.bfloat16)
    return (rows, query, fresh_k, fresh_v)


def attend(query, all_keys, all_values):
    scores = jnp.einsum("qhd,khd->hqk", query, all_keys, preferred_element_type=jnp.float32)
    raised = jnp.exp(scores - jnp.max(scores, axis=-1, keepdims=True))
    weights = (raised / jnp.sum(raised, axis=-1, keepdims=True)).astype(jnp.bfloat16)
    return jnp.einsum("hqk,khd->qhd", weights, all_values, preferred_element_type=jnp.float32)


def per_device(previous, stale_keys, stale_values, modulation, q_gain, k_gain, blocks, refresh):
    state = passed_along(previous, "section", 1)[0].astype(jnp.float32)
    tok_rows = state.shape[0]
    model_width = state.shape[1]
    head_size = q_gain.shape[-1]
    head_count = model_width // head_size
    flags = refresh[0]
    row_flags = jnp.repeat(flags, tok_rows) > 0
    block_count = blocks[0]
    for number in range(stale_keys.shape[1]):
        modulate = modulation[0, number]
        current, query, fresh_k, fresh_v = prepare(
            state, modulate, q_gain[0, number], k_gain[0, number], head_count, head_size
        )
        cache_k = stale_keys[0, number]
        cache_v = stale_values[0, number]
        gathered = lax.all_gather(jnp.stack([fresh_k, fresh_v]), "patch", axis=1, tiled=True)
        all_keys = jnp.where(row_flags[:, None], gathered[0], cache_k)
        all_values = jnp.where(row_flags[:, None], gathered[1], cache_v)
        attended = attend(
            query,
            all_keys.reshape(-1, head_count, head_size),
            all_values.reshape(-1, head_count, head_size),
        )
        attended = attended.reshape(tok_rows, model_width)
        updated = current + modulate[2] * attended
        state = jnp.where(number < block_count, updated, state)
    return state[None]


def solution(mesh):
    placed = (
        P("section", "patch", None),
        P("section", None, None, None),
        P("section", None, None, None),
        P("section", None, None, None),
        P("section", None, None),
        P("section", None, None),
        P("section"),
        P("section", None),
    )
    return jax.shard_map(
        per_device,
        mesh=mesh,
        in_specs=placed,
        out_specs=P("section", "patch", None),
        check_vma=False,
    )
```

profile of v0, /device:TPU:1, one launch (start us, length us, event | category | flops | bytes accessed | tf_op | source)
XLA Modules:
  0.0 127.6 jit_solution(3164465440874473510)
XLA Ops:
  6.5 0.0 all-gather.3.cloned.1.call-start
  6.5 4.0 %collective-permute-start = (bf16[1,16,2048]{2,1,0:T(8,128)(2,1)}, bf16[1,16,2048]{2,1,0:T(8,128)(2,1)S(1)}, u32[]{:S(2)}, u32[]{:S(2)}) collective-permute-start(bf16[1,16,2048]{2,1,0:T(8,128)(2,1)} %param.8), channel_id=1, source_target_pairs={{496,0},{0,16},{16,32},{32,48},{48,64},{64,80},{80,96},{96,112},{1... | collective-permute-start | bytes 196616 | tf_op jit(solution)/shard_map/ppermute | solution.py:14
  10.6 0.8 slice_bitcast_fusion.9
  11.3 0.9 fusion.48
  12.2 4.3 %collective-permute-done = bf16[1,16,2048]{2,1,0:T(8,128)(2,1)S(1)} collective-permute-done((bf16[1,16,2048]{2,1,0:T(8,128)(2,1)}, bf16[1,16,2048]{2,1,0:T(8,128)(2,1)S(1)}, u32[]{:S(2)}, u32[]{:S(2)}) %collective-permute-start) | collective-permute-done | bytes 65568 | tf_op jit(solution)/shard_map/ppermute | solution.py:14
  16.5 0.1 fusion.23
  16.7 0.2 multiply_reduce_fusion.1
  16.9 0.1 copy.33
  17.0 0.1 mul.209.clone
  17.1 0.1 fusion.31
  17.2 0.7 pad_maximum_fusion
  17.9 0.0 all-gather.3.cloned.1.call-update
  17.9 0.0 all-gather.5.cloned.1.call-start
  18.6 0.7 compare_bitcast_fusion
  19.3 0.1 broadcast_in_dim.19
  19.3 0.1 gt.36
  19.4 1.7 %slice_bitcast_fusion.4 = (bf16[32,8,16,128]{3,1,2,0:T(8,128)(2,1)S(1)}, bf16[32,8,16,128]{3,1,2,0:T(8,128)(2,1)S(1)}) fusion(bf16[1,2,256,2048]{3,2,1,0:T(8,128)(2,1)} %param.9), kind=kLoop, calls=%fused_computation.22 | loop fusion | bytes 4194304
  21.1 0.0 copy-start
  21.1 0.2 copy.37
  21.4 1.3 %copy-done = bf16[1,2,256,2048]{3,2,1,0:T(8,128)(2,1)S(1)} copy-done((bf16[1,2,256,2048]{3,2,1,0:T(8,128)(2,1)S(1)}, bf16[1,2,256,2048]{3,2,1,0:T(8,128)(2,1)}, u32[]{:S(2)}) %copy-start) | copy-done | bytes 2097176
  22.7 0.2 slice_bitcast_fusion.7
  22.9 0.0 copy-start.3
  22.9 1.2 copy.39
  24.1 0.0 copy-done.3
  24.1 40.6 %all-gather.3.cloned.1.call-done = bf16[2,256,2048]{2,1,0:T(8,128)(2,1)} async-done(((bf16[2,16,2048]{2,1,0:T(8,128)(2,1)}), bf16[2,256,2048]{2,1,0:T(8,128)(2,1)}) %all-gather.3.cloned.1.call-update) | async-done | bytes 2097168 | tf_op jit(solution)/shard_map/all_gather | solution.py:54
  64.8 1.7 %slice_bitcast_fusion.3 = (bf16[32,8,16,128]{3,1,2,0:T(8,128)(2,1)S(1)}, bf16[32,8,16,128]{3,1,2,0:T(8,128)(2,1)S(1)}) fusion(bf16[2,256,2048]{2,1,0:T(8,128)(2,1)} %all-gather.3.cloned.1.call-done), kind=kLoop, calls=%fused_computation.10 | loop fusion | bytes 4194304
  66.5 0.2 copy.36
  66.7 1.2 copy.38
  67.9 0.7 fusion.9
  68.6 0.0 copy-start.2
  68.6 0.2 fusion.49
  68.8 0.5 copy-done.2
  69.3 2.6 %fusion.11 = f32[16,128,16]{1,2,0:T(8,128)S(1)} fusion(bf16[256,16,128]{2,1,0:T(8,128)(2,1)} %bitcast.102, bf16[256,16,128]{2,1,0:T(8,128)(2,1)} %bitcast.105, pred[256]{0:T(512)(128)(4,1)S(1)} %gt.36, f32[16,16]{1,0:T(8,128)S(1)} %fusion.49, f32[16,16,256]{2,1,0:T(8,128)} %copy-done.2), kind=kOutput, calls=%fused_computation.20 | convolution fusion | flops 17498624 | bytes 2491648 | tf_op jit(solution)/shard_map/hqk,khd->qhd/dot_general | solution.py:35
  71.9 0.1 fusion.25
  72.1 0.2 multiply_reduce_fusion
  72.3 0.1 multiply_convert_fusion.1
  72.5 0.1 add_convert_fusion
  72.6 0.7 pad_maximum_fusion.1
  73.3 0.0 all-gather.5.cloned.1.call-update
  73.3 0.2 copy.41
  73.6 0.2 copy.43
  73.8 41.0 %all-gather.5.cloned.1.call-done = bf16[2,256,2048]{2,1,0:T(8,128)(2,1)} async-done(((bf16[2,16,2048]{2,1,0:T(8,128)(2,1)}), bf16[2,256,2048]{2,1,0:T(8,128)(2,1)}) %all-gather.5.cloned.1.call-update) | async-done | bytes 2097168 | tf_op jit(solution)/shard_map/all_gather | solution.py:54
  114.8 1.7 %slice_bitcast_fusion.1 = (bf16[32,8,16,128]{3,1,2,0:T(8,128)(2,1)S(1)}, bf16[32,8,16,128]{3,1,2,0:T(8,128)(2,1)S(1)}) fusion(bf16[2,256,2048]{2,1,0:T(8,128)(2,1)} %all-gather.5.cloned.1.call-done), kind=kLoop, calls=%fused_computation.8 | loop fusion | bytes 4194304
  116.5 0.2 copy.40
  116.7 0.7 fusion.6
  117.3 0.0 copy-start.1
  117.3 0.2 fusion.50
  117.5 0.2 copy.42
  117.8 0.3 copy-done.1
  118.0 1.9 %convolution_bitcast_fusion = f32[16,16,128]{2,0,1:T(8,128)S(1)} fusion(bf16[256,16,128]{2,1,0:T(8,128)(2,1)S(1)} %bitcast.103, bf16[256,16,128]{2,1,0:T(8,128)(2,1)S(1)} %bitcast.108, pred[256]{0:T(512)(128)(4,1)S(1)} %gt.36, f32[16,16]{1,0:T(8,128)S(1)} %fusion.50, f32[16,16,256]{2,1,0:T(8,128)} %copy-done.1), kind=kOutput, calls=%fused_computation.6 | convolution fusion | flops 17498624 | bytes 2491648 | tf_op jit(solution)/shard_map/hqk,khd->qhd/dot_general | solution.py:35
  120.0 0.7 add_select_fusion
  (15 shorter events, 0.3 us)
Async XLA Ops:
  6.5 58.2 %all-gather.3.cloned.1.call-start = ((), (), s32[]{:S(2)}) async-start(), calls=%async_computation | async-start | bytes 2228224 | tf_op jit(solution)/shard_map/all_gather | solution.py:54
  6.5 10.0 %collective-permute-start = (bf16[1,16,2048]{2,1,0:T(8,128)(2,1)}, bf16[1,16,2048]{2,1,0:T(8,128)(2,1)S(1)}, u32[]{:S(2)}, u32[]{:S(2)}) collective-permute-start(bf16[1,16,2048]{2,1,0:T(8,128)(2,1)} %param.8), channel_id=1, source_target_pairs={{496,0},{0,16},{16,32},{32,48},{48,64},{64,80},{80,96},{96,112},{1... | collective-permute-start | bytes 196616 | tf_op jit(solution)/shard_map/ppermute | solution.py:14
  17.9 96.9 %all-gather.5.cloned.1.call-start = ((), (), s32[]{:S(2)}) async-start(), calls=%async_computation.1 | async-start | bytes 2228224 | tf_op jit(solution)/shard_map/all_gather | solution.py:54
  21.1 1.6 %copy-start = (bf16[1,2,256,2048]{3,2,1,0:T(8,128)(2,1)S(1)}, bf16[1,2,256,2048]{3,2,1,0:T(8,128)(2,1)}, u32[]{:S(2)}) copy-start(bf16[1,2,256,2048]{3,2,1,0:T(8,128)(2,1)} %param.10) | copy-start | bytes 6291460
  22.9 1.2 copy-start.3
  68.6 0.7 copy-start.2
  117.3 0.7 copy-start.1
Sparse Core Ops, SparseCore 0:
  18.0 46.7 all-gather.2
  73.4 41.2 all-gather.4
where the time goes:
time: 128 us
  waiting for transfers between devices  86 us (67%)
  between operations  14.3 us (11%)
  local copies, waits for them, and re-layouts  12.5 us (10%)
  matrix products  5.81 us (5%)
  other arithmetic  4.92 us (4%)
  starting transfers between devices  4.07 us (3%)
    all_gather x2, waiting for transfers between devices, per_device(): lax.all_gather(jnp.stack([fresh_k, fresh_v]), 'patch', axis=1, tiled=True)  81.6 us
    unnamed x22, local copies, waits for them, and re-layouts  11.3 us
    dot_general x2, matrix products, attend(): jnp.einsum('hqk,khd->qhd', weights, all_values, preferred_element_type=jn...  4.49 us
    ppermute x1, waiting for transfers between devices, passed_along(): return lax.ppermute(block, axis, route)  4.31 us
    ppermute x1, starting transfers between devices, passed_along(): return lax.ppermute(block, axis, route)  4.02 us
  transfers between devices with their start and end apart: 3, of which 3 were waited for; matrix products, arithmetic and copies ran while one was open for 5% of the time, Pallas kernels for 0%

commit v1 on v0

v1 whole, which is shorter than its diff:
```python
import functools
import math

import jax
import jax.numpy as jnp
from jax import lax
from jax.experimental import pallas as pl
from jax.experimental.pallas import tpu as pltpu
from jax.sharding import PartitionSpec as P

epsilon = 1e-06
VMEM_BYTES = 60 * 2**20
MESH = pl.DeviceIdType.MESH


def spread_order(count):
    chips = count // 2
    order = []
    for distance in range(chips // 2, 0, -1):
        order.append(distance)
        if chips - distance != distance:
            order.append(chips - distance)
    order.append(0)
    return [(2 * step, flip) for step in order for flip in (0, 1)]


def kernel(
    sections, patches, previous, stale_k, stale_v, modulation, q_gain, k_gain, blocks, refresh, out,
    own_rows, own_inv, state_in, inv_in, cache_k, cache_v, mod, qg, kg, flags, count,
    own_sums, sums_in, result, load_sem, send_sem, recv_sem,
):
    section = lax.axis_index("section")
    patch = lax.axis_index("patch")
    after = lax.rem(section + 1, sections)
    before = lax.rem(section + sections - 1, sections)
    tok_rows, width = own_rows.shape
    tokens, head = state_in.shape
    column = pl.ds(pl.multiple_of(patch * head, head), head)
    rows_here = pl.ds(pl.multiple_of(patch * tok_rows, tok_rows), tok_rows)

    partners = []
    for step, flip in spread_order(patches):
        chip = lax.rem(patch // 2 * 2 + step, patches)
        core = lax.rem(patch + flip, 2)
        partners.append(chip + core)

    barrier = pltpu.get_barrier_semaphore()
    for partner in partners:
        pl.semaphore_signal(
            barrier, inc=1, device_id={"section": before, "patch": partner}, device_id_type=MESH
        )

    loads = [
        pltpu.make_async_copy(previous.at[0], own_rows, load_sem.at[0]),
        pltpu.make_async_copy(stale_k.at[0, :, :, column], cache_k, load_sem.at[1]),
        pltpu.make_async_copy(stale_v.at[0, :, :, column], cache_v, load_sem.at[2]),
        pltpu.make_async_copy(modulation.at[0, :, :, column], mod, load_sem.at[3]),
        pltpu.make_async_copy(q_gain.at[0], qg, load_sem.at[4]),
        pltpu.make_async_copy(k_gain.at[0], kg, load_sem.at[5]),
        pltpu.make_async_copy(refresh, flags, load_sem.at[7]),
        pltpu.make_async_copy(blocks, count, load_sem.at[8]),
    ]
    for load in loads:
        load.start()

    lane = lax.broadcasted_iota(jnp.int32, (tok_rows, head), 1)
    row = lax.broadcasted_iota(jnp.int32, (tok_rows, head), 0)
    loads[0].wait()
    rows = own_rows[...].astype(jnp.float32)
    inverse = lax.rsqrt(jnp.mean(rows * rows, axis=-1, keepdims=True) + epsilon)
    own_inv[...] = jnp.sum(jnp.where(lane == row, inverse, 0.0), axis=0, keepdims=True)

    pl.semaphore_wait(barrier, patches)

    sends = []
    for partner in partners:
        target = {"section": after, "patch": partner}
        sends.append(pltpu.make_async_remote_copy(
            src_ref=own_inv, dst_ref=inv_in.at[patch], send_sem=send_sem.at[0], recv_sem=recv_sem.at[0],
            device_id=target, device_id_type=MESH,
        ))
        sends.append(pltpu.make_async_remote_copy(
            src_ref=own_rows.at[:, pl.ds(pl.multiple_of(partner * head, head), head)],
            dst_ref=state_in.at[rows_here, :], send_sem=send_sem.at[1], recv_sem=recv_sem.at[1],
            device_id=target, device_id_type=MESH,
        ))
    for send in sends:
        send.start()

    for load in loads[1:]:
        load.wait()
    flag_lane = lax.broadcasted_iota(jnp.int32, (tokens, patches), 1)
    flag_row = lax.broadcasted_iota(jnp.int32, (tokens, patches), 0)
    fresh = jnp.sum(
        jnp.where(flag_lane == flag_row // tok_rows, flags[...].astype(jnp.float32), 0.0), axis=-1, keepdims=True
    ) > 0.5

    def block(state, inverse, number):
        modded = state * inverse * (1.0 + mod[1, number:number + 1]) + mod[0, number:number + 1]
        normed = modded * lax.rsqrt(jnp.mean(modded * modded, axis=-1, keepdims=True) + epsilon)
        query = (normed * qg[number:number + 1] * (1.0 / math.sqrt(head))).astype(jnp.bfloat16)
        fresh_k = normed * kg[number:number + 1]
        all_keys = jnp.where(fresh, fresh_k, cache_k[number].astype(jnp.float32)).astype(jnp.bfloat16)
        all_values = jnp.where(fresh, modded, cache_v[number].astype(jnp.float32)).astype(jnp.bfloat16)
        scores = lax.dot_general(
            query, all_keys, (((1,), (1,)), ((), ())), preferred_element_type=jnp.float32
        )
        raised = jnp.exp(scores - jnp.max(scores, axis=-1, keepdims=True))
        weights = (raised / jnp.sum(raised, axis=-1, keepdims=True)).astype(jnp.bfloat16)
        attended = jnp.dot(weights, all_values, preferred_element_type=jnp.float32)
        updated = state + mod[2, number:number + 1] * attended
        return jnp.where(count[...] > number, updated, state)

    pltpu.make_async_copy(inv_in, inv_in, recv_sem.at[0]).wait()
    pltpu.make_async_copy(state_in, state_in, recv_sem.at[1]).wait()
    state = state_in[...].astype(jnp.float32)
    spread = jnp.broadcast_to(inv_in[...], (patches, tok_rows, head))
    inverse = jnp.sum(jnp.where((lane == row)[None], spread, 0.0), axis=-1, keepdims=True).reshape(tokens, 1)
    state = block(state, inverse, 0)

    halves = tokens // head
    lanes = lax.broadcasted_iota(jnp.int32, (head, head), 1)
    diagonal = (lanes == lax.broadcasted_iota(jnp.int32, (head, head), 0))[None]
    sums = jnp.sum(state * state, axis=-1, keepdims=True).reshape(halves, head, 1)
    own_sums[...] = jnp.sum(jnp.where(diagonal, sums, 0.0), axis=1)
    for partner in partners[:-2] + partners[-1:]:
        send = pltpu.make_async_remote_copy(
            src_ref=own_sums, dst_ref=sums_in.at[patch], send_sem=send_sem.at[2], recv_sem=recv_sem.at[2],
            device_id={"patch": partner}, device_id_type=MESH,
        )
        send.start()
    sums_in[patch] = own_sums[...]
    others = sums_in.at[pl.ds(0, patches - 1)]
    pltpu.make_async_copy(others, others, recv_sem.at[2]).wait()
    total = jnp.sum(sums_in[...], axis=0)
    spread = jnp.broadcast_to(total[:, None, :], (halves, head, head))
    total = jnp.sum(jnp.where(diagonal, spread, 0.0), axis=-1, keepdims=True).reshape(tokens, 1)
    inverse = lax.rsqrt(total * (1.0 / width) + epsilon)
    state = block(state, inverse, 1)

    result[...] = state.astype(result.dtype)
    for partner in partners[:-2] + partners[-1:]:
        send = pltpu.make_async_remote_copy(
            src_ref=result.at[pl.ds(pl.multiple_of(partner * tok_rows, tok_rows), tok_rows), :],
            dst_ref=out.at[:, column], send_sem=send_sem.at[3], recv_sem=recv_sem.at[3],
            device_id={"patch": partner}, device_id_type=MESH,
        )
        send.start()
    own = pltpu.make_async_copy(result.at[rows_here, :], out.at[:, column], load_sem.at[6])
    own.start()
    own.wait()
    pltpu.make_async_copy(inv_in, inv_in, send_sem.at[0]).wait()
    pltpu.make_async_copy(state_in, state_in, send_sem.at[1]).wait()
    pltpu.make_async_copy(others, others, send_sem.at[2]).wait()
    rest = result.at[pl.ds(0, tokens - tok_rows), :]
    pltpu.make_async_copy(rest, rest, send_sem.at[3]).wait()
    pltpu.make_async_copy(rest, rest, recv_sem.at[3]).wait()


def per_device(previous, stale_keys, stale_values, modulation, q_gain, k_gain, blocks, refresh):
    sections = lax.axis_size("section")
    patches = lax.axis_size("patch")
    _, tok_rows, width = previous.shape
    _, layers, tokens, _ = stale_keys.shape
    head = q_gain.shape[-1]
    anywhere = pl.BlockSpec(memory_space=pl.ANY)
    mixed = pl.pallas_call(
        functools.partial(kernel, sections, patches),
        out_shape=jax.ShapeDtypeStruct((tok_rows, width), jnp.bfloat16),
        in_specs=[anywhere] * 8,
        out_specs=pl.BlockSpec(memory_space=pltpu.VMEM),
        scratch_shapes=[
            pltpu.VMEM((tok_rows, width), jnp.bfloat16),
            pltpu.VMEM((1, head), jnp.float32),
            pltpu.VMEM((tokens, head), jnp.bfloat16),
            pltpu.VMEM((patches, 1, head), jnp.float32),
            pltpu.VMEM((layers, tokens, head), jnp.bfloat16),
            pltpu.VMEM((layers, tokens, head), jnp.bfloat16),
            pltpu.VMEM((3, layers, head), jnp.float32),
            pltpu.VMEM((layers, head), jnp.float32),
            pltpu.VMEM((layers, head), jnp.float32),
            pltpu.VMEM((1, patches), jnp.int32),
            pltpu.VMEM((1, 1), jnp.int32),
            pltpu.VMEM((tokens // head, head), jnp.float32),
            pltpu.VMEM((patches, tokens // head, head), jnp.float32),
            pltpu.VMEM((tokens, head), jnp.bfloat16),
            pltpu.SemaphoreType.DMA((9,)),
            pltpu.SemaphoreType.DMA((4,)),
            pltpu.SemaphoreType.DMA((4,)),
        ],
        compiler_params=pltpu.CompilerParams(collective_id=0, has_side_effects=True, vmem_limit_bytes=VMEM_BYTES),
    )(previous, stale_keys, stale_values, jnp.swapaxes(modulation, 1, 2), q_gain, k_gain, blocks[None], refresh)
    return mixed.astype(jnp.float32)[None]


def solution(mesh):
    placed = (
        P("section", "patch", None),
        P("section", None, None, None),
        P("section", None, None, None),
        P("section", None, None, None),
        P("section", None, None),
        P("section", None, None),
        P("section"),
        P("section", None),
    )
    return jax.shard_map(
        per_device,
        mesh=mesh,
        in_specs=placed,
        out_specs=P("section", "patch", None),
        check_vma=False,
    )
```

time: 128 us -> 34.2 us (0.27)
  waiting for transfers between devices: 86 us -> 0 us
  Pallas kernels: 0 us -> 31.8 us
  between operations: 14.3 us -> 0.66 us
  local copies, waits for them, and re-layouts: 12.5 us -> 0 us
  matrix products: 5.81 us -> 0 us
  starting transfers between devices: 4.07 us -> 0 us
  other arithmetic: 4.92 us -> 1.5 us
    all_gather x2 -> x0, waiting for transfers between devices: 81.6 us -> none  [per_device(): lax.all_gather(jnp.stack([fresh_k, fresh_v]), 'patch', axis=1, tiled=True)]
    pallas_call x0 -> x1, Pallas kernels: none -> 31.8 us  [per_device(): pl.pallas_call(functools.partial(kernel, sections, patches), out_shape=ja...]
    unnamed x22 -> x0, local copies, waits for them, and re-layouts: 11.3 us -> none
    dot_general x4 -> x0, matrix products: 5.81 us -> none  [the longest x2 4.49 us: attend(): jnp.einsum('hqk,khd->qhd', weights, all_values, preferred_element_type=jn...]
    ppermute x1 -> x0, waiting for transfers between devices: 4.31 us -> none  [passed_along(): return lax.ppermute(block, axis, route)]
    ppermute x1 -> x0, starting transfers between devices: 4.02 us -> none  [passed_along(): return lax.ppermute(block, axis, route)]
    broadcast_in_dim x0 -> x1, other arithmetic: none -> 1.5 us  [per_device(): return mixed.astype(jnp.float32)[None]]
    another operation x2 -> x0, other arithmetic: 1.34 us -> none  [per_device(): jnp.stack([fresh_k, fresh_v])]
  transfers between devices with their start and end apart: 3 -> 0, of which waited for: 3 -> 0; matrix products, arithmetic and copies ran while one was open for 5% -> 0% of each run, Pallas kernels for 0% -> 0%
where the time goes in v1:
time: 34.2 us; the launch traced here: 34 us
  Pallas kernels  31.8 us (93%)
  other arithmetic  1.5 us (4%)
  between operations  0.66 us (2%)
    pallas_call x1, Pallas kernels, per_device(): pl.pallas_call(functools.partial(kernel, sections, patches), out_shape=ja...  31.8 us
    broadcast_in_dim x1, other arithmetic, per_device(): return mixed.astype(jnp.float32)[None]  1.5 us

profile of v1, /device:TPU:1, one launch (start us, length us, event | category | flops | bytes accessed | tf_op | source)
XLA Modules:
  0.0 34.0 jit_solution(8522502381738990661)
XLA Ops:
  0.7 31.8 %shard_map.82 = bf16[16,2048]{1,0:T(8,128)(2,1)} custom-call(bf16[1,16,2048]{2,1,0:T(8,128)(2,1)} %previous.1, bf16[1,2,256,2048]{3,2,1,0:T(8,128)(2,1)} %stale_k.1, bf16[1,2,256,2048]{3,2,1,0:T(8,128)(2,1)} %stale_v.1, f32[1,3,2,2048]{3,2,1,0:T(2,128)} %bitcast.6, f32[1,2,128]{2,1,0:T(2,128)} %q_gain.1, f32[1,2,128]{2,1,0:T(2,128)} %k_gain.1, ...), custom_call_target="tpu_custom_call" | custom-call | tf_op jit(solution)/shard_map/pallas_call | solution.py:167
  32.5 1.5 %bitcast_convert_fusion = f32[1,16,2048]{2,1,0:T(8,128)} fusion(bf16[16,2048]{1,0:T(8,128)(2,1)} %shard_map.82), kind=kLoop, calls=%fused_computation | loop fusion | flops 32768 | bytes 196608 | tf_op jit(solution)/shard_map/broadcast_in_dim | solution.py:193

commit v2 on v0

v2 whole, which is shorter than its diff:
```python
import functools
import math

import jax
import jax.numpy as jnp
from jax import lax
from jax.experimental import pallas as pl
from jax.experimental.pallas import tpu as pltpu
from jax.sharding import PartitionSpec as P

epsilon = 1e-06
VMEM_BYTES = 48 * 2**20
MESH = pl.DeviceIdType.MESH
PIECES = 2
FIRST, WORKERS = 2, 4


def kernel(
    sections, patches, head, previous, stale_k, stale_v, modulation, q_gain, k_gain, refresh, blocks, out,
    own_rows, own_inv, state_in, inv_in, cache_k, cache_v, mod, qg, kg, flags, count,
    own_sums, sums_in, result, load_sem, send_sem, recv_sem, ready_sem,
):
    section = lax.axis_index("section")
    patch = lax.axis_index("patch")
    after = lax.rem(section + 1, sections)
    before = lax.rem(section + sections - 1, sections)
    tok_rows, width = own_rows.shape
    tokens, part = state_in.shape
    share = part // PIECES
    works = jnp.logical_and(patch >= FIRST, patch < FIRST + WORKERS)
    slot = lax.rem(patch + patches - FIRST, patches)
    mine = lax.rem(slot, WORKERS)
    column = pl.ds(pl.multiple_of(mine * part, part), part)
    rows_here = pl.ds(pl.multiple_of(patch * tok_rows, tok_rows), tok_rows)

    barrier = pltpu.get_barrier_semaphore()

    def to(where, partner):
        return {"device_id": {"section": where, "patch": partner}, "device_id_type": MESH}

    loads = [
        pltpu.make_async_copy(stale_k.at[0, :, :, column], cache_k, load_sem.at[1]),
        pltpu.make_async_copy(stale_v.at[0, :, :, column], cache_v, load_sem.at[2]),
        pltpu.make_async_copy(modulation.at[0, :, :, column], mod, load_sem.at[3]),
        pltpu.make_async_copy(q_gain.at[0], qg, load_sem.at[4]),
        pltpu.make_async_copy(k_gain.at[0], kg, load_sem.at[5]),
        pltpu.make_async_copy(refresh, flags, load_sem.at[6]),
        pltpu.make_async_copy(blocks, count, load_sem.at[7]),
    ]
    load_rows = pltpu.make_async_copy(previous.at[0], own_rows, load_sem.at[0])
    load_rows.start()

    @pl.when(works)
    def _():
        for partner in range(patches - 1, -1, -1):
            pl.semaphore_signal(barrier, inc=1, **to(before, partner))
        for partner in range(patches - 1, -1, -1):
            @pl.when(partner != patch)
            def _():
                pl.semaphore_signal(barrier, inc=1, **to(section, partner))
        for load in loads:
            load.start()

    pl.semaphore_wait(barrier, 2 * WORKERS - works.astype(jnp.int32))

    def pass_on(piece):
        for index in range(WORKERS):
            pltpu.make_async_remote_copy(
                src_ref=previous.at[0, :, pl.ds(index * part + piece * share, share)],
                dst_ref=state_in.at[rows_here, pl.ds(piece * share, share)],
                send_sem=send_sem.at[1], recv_sem=recv_sem.at[4 + piece], **to(after, FIRST + index),
            ).start()

    pass_on(0)
    load_rows.wait()
    rows = own_rows[...].astype(jnp.float32)
    lane = lax.broadcasted_iota(jnp.int32, (tok_rows, 128), 1)
    row = lax.broadcasted_iota(jnp.int32, (tok_rows, 128), 0)
    inverse = lax.rsqrt(jnp.mean(rows * rows, axis=-1, keepdims=True) + epsilon)
    own_inv[...] = jnp.sum(jnp.where(lane == row, inverse, 0.0), axis=0, keepdims=True)
    for index in range(WORKERS):
        pltpu.make_async_remote_copy(
            src_ref=own_inv, dst_ref=inv_in.at[patch],
            send_sem=send_sem.at[0], recv_sem=recv_sem.at[0], **to(after, FIRST + index),
        ).start()
    for piece in range(1, PIECES):
        pass_on(piece)

    @pl.when(jnp.logical_not(works))
    def _():
        for index in range(WORKERS):
            pl.semaphore_signal(ready_sem, inc=1, **to(section, FIRST + index))

    @pl.when(works)
    def _():
        flag_lane = lax.broadcasted_iota(jnp.int32, (tokens, patches), 1)
        flag_row = lax.broadcasted_iota(jnp.int32, (tokens, patches), 0)
        for load in loads:
            load.wait()
        fresh = jnp.sum(
            jnp.where(flag_lane == flag_row // tok_rows, flags[...].astype(jnp.float32), 0.0), axis=-1, keepdims=True
        ) > 0.5

        def prepare(h, state, inverse, number):
            here = slice(h * head, (h + 1) * head)
            modded = state * inverse * (1.0 + mod[1, number:number + 1, here]) + mod[0, number:number + 1, here]
            normed = modded * lax.rsqrt(jnp.mean(modded * modded, axis=-1, keepdims=True) + epsilon)
            query = (normed * (qg[number:number + 1] * (1.0 / math.sqrt(head)))).astype(jnp.bfloat16)
            cached_k = cache_k[number, :, here].astype(jnp.float32)
            cached_v = cache_v[number, :, here].astype(jnp.float32)
            all_keys = jnp.where(fresh, normed * kg[number:number + 1], cached_k).astype(jnp.bfloat16)
            all_values = jnp.where(fresh, modded, cached_v).astype(jnp.bfloat16)
            return query, all_keys, all_values

        def attend(h, state, number, query, all_keys, all_values):
            here = slice(h * head, (h + 1) * head)
            scores = lax.dot_general(
                query, all_keys, (((1,), (1,)), ((), ())), preferred_element_type=jnp.float32
            )
            raised = jnp.exp(scores - jnp.max(scores, axis=-1, keepdims=True))
            total = jnp.sum(raised, axis=-1, keepdims=True)
            weights = (raised * (1.0 / total)).astype(jnp.bfloat16)
            attended = jnp.dot(weights, all_values, preferred_element_type=jnp.float32)
            updated = state + mod[2, number:number + 1, here] * attended
            return jnp.where(count[...] > number, updated, state)

        pltpu.make_async_copy(inv_in, inv_in, recv_sem.at[0]).wait()
        spread = jnp.broadcast_to(inv_in[...], (patches, tok_rows, 128))
        inverse = jnp.sum(jnp.where((lane == row)[None], spread, 0.0), axis=-1, keepdims=True).reshape(tokens, 1)
        heads = part // head
        middle = []
        for piece in range(PIECES):
            arrived = state_in.at[:, pl.ds(piece * share, share)]
            pltpu.make_async_copy(arrived, arrived, recv_sem.at[4 + piece]).wait()
            for h in range(piece * heads // PIECES, (piece + 1) * heads // PIECES):
                state = state_in[:, h * head:(h + 1) * head].astype(jnp.float32)
                middle.append(attend(h, state, 0, *prepare(h, state, inverse, 0)))

        halves = tokens // 128
        lanes = lax.broadcasted_iota(jnp.int32, (128, 128), 1)
        diagonal = (lanes == lax.broadcasted_iota(jnp.int32, (128, 128), 0))[None]
        squares = functools.reduce(jnp.add, [state * state for state in middle])
        sums = jnp.sum(squares, axis=-1, keepdims=True).reshape(halves, 128, 1)
        own_sums[...] = jnp.sum(jnp.where(diagonal, sums, 0.0), axis=1)
        for step in range(1, WORKERS):
            pltpu.make_async_remote_copy(
                src_ref=own_sums, dst_ref=sums_in.at[slot], send_sem=send_sem.at[2], recv_sem=recv_sem.at[2],
                **to(section, FIRST + lax.rem(slot + step, WORKERS)),
            ).start()
        sums_in[slot] = own_sums[...]
        others = sums_in.at[pl.ds(0, WORKERS - 1)]
        pltpu.make_async_copy(others, others, recv_sem.at[2]).wait()
        total = jnp.sum(sums_in[...], axis=0)
        spread = jnp.broadcast_to(total[:, None, :], (halves, 128, 128))
        total = jnp.sum(jnp.where(diagonal, spread, 0.0), axis=-1, keepdims=True).reshape(tokens, 1)
        inverse = lax.rsqrt(total * (1.0 / width) + epsilon)

        pl.semaphore_wait(ready_sem, patches - WORKERS)

        def give(partner, first, last):
            rows_there = pl.ds(partner * tok_rows, tok_rows)
            source = result.at[rows_there, pl.ds(first * head, (last - first) * head)]
            target = out.at[:, pl.ds(pl.multiple_of(mine * part + first * head, head), (last - first) * head)]

            def send():
                pltpu.make_async_remote_copy(
                    src_ref=source, dst_ref=target, send_sem=send_sem.at[3], recv_sem=recv_sem.at[3],
                    **to(section, partner),
                ).start()

            if FIRST <= partner < FIRST + WORKERS:
                pl.when(partner != patch)(send)

                @pl.when(partner == patch)
                def _():
                    pltpu.make_async_copy(source, target, load_sem.at[8]).start()
            else:
                send()

        ready = [prepare(h, middle[h], inverse, 1) for h in range(heads)]
        for first, last in ((0, tokens // 2), (tokens // 2, tokens)):
            for h in range(heads):
                query, all_keys, all_values = ready[h]
                state = attend(h, middle[h][first:last], 1, query[first:last], all_keys, all_values)
                result[first:last, h * head:(h + 1) * head] = state.astype(result.dtype)
                if first == 0:
                    for partner in range(FIRST):
                        give(partner, h, h + 1)
            for partner in range(max(first // tok_rows, FIRST), last // tok_rows):
                give(partner, 0, heads)
        pltpu.make_async_copy(result.at[rows_here, :], out.at[:, column], load_sem.at[8]).wait()
        pltpu.make_async_copy(others, others, send_sem.at[2]).wait()
        rest = result.at[pl.ds(0, tokens - tok_rows), :]
        pltpu.make_async_copy(rest, rest, send_sem.at[3]).wait()
        arriving = out.at[:, pl.ds(0, width - part)]
        pltpu.make_async_copy(arriving, arriving, recv_sem.at[3]).wait()

    sent = inv_in.at[pl.ds(0, WORKERS)]
    pltpu.make_async_copy(sent, sent, send_sem.at[0]).wait()
    pltpu.make_async_copy(own_rows, own_rows, send_sem.at[1]).wait()

    @pl.when(jnp.logical_not(works))
    def _():
        pltpu.make_async_copy(out, out, recv_sem.at[3]).wait()


def per_device(previous, stale_keys, stale_values, modulation, q_gain, k_gain, blocks, refresh):
    sections = lax.axis_size("section")
    patches = lax.axis_size("patch")
    _, tok_rows, width = previous.shape
    _, layers, tokens, _ = stale_keys.shape
    head = q_gain.shape[-1]
    part = width // WORKERS
    anywhere = pl.BlockSpec(memory_space=pl.ANY)
    operands = (previous, stale_keys, stale_values, jnp.swapaxes(modulation, 1, 2), q_gain, k_gain, refresh)
    stay = [pltpu.with_memory_space_constraint(operand, pltpu.HBM) for operand in operands]
    mixed = pl.pallas_call(
        functools.partial(kernel, sections, patches, head),
        out_shape=pltpu.VMEM((tok_rows, width), jnp.bfloat16),
        in_specs=[anywhere] * 8,
        out_specs=pl.BlockSpec(memory_space=pltpu.VMEM),
        scratch_shapes=[
            pltpu.VMEM((tok_rows, width), jnp.bfloat16),
            pltpu.VMEM((1, 128), jnp.float32),
            pltpu.VMEM((tokens, part), jnp.bfloat16),
            pltpu.VMEM((patches, 1, 128), jnp.float32),
            pltpu.VMEM((layers, tokens, part), jnp.bfloat16),
            pltpu.VMEM((layers, tokens, part), jnp.bfloat16),
            pltpu.VMEM((3, layers, part), jnp.float32),
            pltpu.VMEM((layers, head), jnp.float32),
            pltpu.VMEM((layers, head), jnp.float32),
            pltpu.VMEM((1, patches), jnp.int32),
            pltpu.VMEM((1, 1), jnp.int32),
            pltpu.VMEM((tokens // 128, 128), jnp.float32),
            pltpu.VMEM((WORKERS, tokens // 128, 128), jnp.float32),
            pltpu.VMEM((tokens, part), jnp.bfloat16),
            pltpu.SemaphoreType.DMA((9,)),
            pltpu.SemaphoreType.DMA((4,)),
            pltpu.SemaphoreType.DMA((4 + PIECES,)),
            pltpu.SemaphoreType.REGULAR,
        ],
        compiler_params=pltpu.CompilerParams(
            collective_id=0, has_side_effects=True, vmem_limit_bytes=VMEM_BYTES
        ),
    )(*stay, blocks[None])
    return mixed.astype(jnp.float32)[None]


def solution(mesh):
    placed = (
        P("section", "patch", None),
        P("section", None, None, None),
        P("section", None, None, None),
        P("section", None, None, None),
        P("section", None, None),
        P("section", None, None),
        P("section"),
        P("section", None),
    )
    return jax.shard_map(
        per_device,
        mesh=mesh,
        in_specs=placed,
        out_specs=P("section", "patch", None),
        check_vma=False,
    )
```

time: 128 us -> 31.2 us (0.24)
  waiting for transfers between devices: 86 us -> 0 us
  Pallas kernels: 0 us -> 29.7 us
  between operations: 14.3 us -> 0.66 us
  local copies, waits for them, and re-layouts: 12.5 us -> 0 us
  matrix products: 5.81 us -> 0 us
  other arithmetic: 4.92 us -> 0.67 us
  starting transfers between devices: 4.07 us -> 0 us
    all_gather x2 -> x0, waiting for transfers between devices: 81.6 us -> none  [per_device(): lax.all_gather(jnp.stack([fresh_k, fresh_v]), 'patch', axis=1, tiled=True)]
    pallas_call x0 -> x1, Pallas kernels: none -> 29.7 us  [per_device(): pl.pallas_call(functools.partial(kernel, sections, patches, head), out_sh...]
    unnamed x22 -> x0, local copies, waits for them, and re-layouts: 11.3 us -> none
    dot_general x4 -> x0, matrix products: 5.81 us -> none  [the longest x2 4.49 us: attend(): jnp.einsum('hqk,khd->qhd', weights, all_values, preferred_element_type=jn...]
    ppermute x1 -> x0, waiting for transfers between devices: 4.31 us -> none  [passed_along(): return lax.ppermute(block, axis, route)]
    ppermute x1 -> x0, starting transfers between devices: 4.02 us -> none  [passed_along(): return lax.ppermute(block, axis, route)]
    another operation x2 -> x0, other arithmetic: 1.34 us -> none  [per_device(): jnp.stack([fresh_k, fresh_v])]
  transfers between devices with their start and end apart: 3 -> 0, of which waited for: 3 -> 0; matrix products, arithmetic and copies ran while one was open for 5% -> 0% of each run, Pallas kernels for 0% -> 0%
where the time goes in v2:
time: 31.2 us; the launch traced here: 31.1 us
  Pallas kernels  29.7 us (95%)
  other arithmetic  0.67 us (2%)
  between operations  0.66 us (2%)
    pallas_call x1, Pallas kernels, per_device(): pl.pallas_call(functools.partial(kernel, sections, patches, head), out_sh...  29.7 us
    broadcast_in_dim x1, other arithmetic, per_device(): return mixed.astype(jnp.float32)[None]  0.67 us

profile of v2, /device:TPU:1, one launch (start us, length us, event | category | flops | bytes accessed | tf_op | source)
XLA Modules:
  0.0 31.1 jit_solution(10598185522067651224)
XLA Ops:
  0.7 29.7 %shard_map.82 = bf16[16,2048]{1,0:T(8,128)(2,1)S(1)} custom-call(bf16[1,16,2048]{2,1,0:T(8,128)(2,1)} %previous.1, bf16[1,2,256,2048]{3,2,1,0:T(8,128)(2,1)} %stale_k.1, bf16[1,2,256,2048]{3,2,1,0:T(8,128)(2,1)} %stale_v.1, f32[1,3,2,2048]{3,2,1,0:T(2,128)} %bitcast.6, f32[1,2,128]{2,1,0:T(2,128)} %q_gain.1, f32[1,2,128]{2,1,0:T(2,128)} %k_gain.1, ...), custom_call_target="tpu_custom_call" | custom-call | tf_op jit(solution)/shard_map/pallas_call | solution.py:217
  30.4 0.7 %bitcast_convert_fusion = f32[1,16,2048]{2,1,0:T(8,128)} fusion(bf16[16,2048]{1,0:T(8,128)(2,1)S(1)} %shard_map.82), kind=kLoop, calls=%fused_computation | loop fusion | flops 32768 | bytes 196608 | tf_op jit(solution)/shard_map/broadcast_in_dim | solution.py:246

commit v3 on v2

--- a/solution.py
+++ b/solution.py
@@ -12,6 +12,7 @@
 VMEM_BYTES = 48 * 2**20
 MESH = pl.DeviceIdType.MESH
 PIECES = 2
+STEPS = ((0, 256, (1, 3, 2, 0, 4, 5, 6, 7, 14, 15, 8, 9, 12, 13, 10, 11)),)
 FIRST, WORKERS = 2, 4
 
 
@@ -48,7 +49,6 @@
         pltpu.make_async_copy(blocks, count, load_sem.at[7]),
     ]
     load_rows = pltpu.make_async_copy(previous.at[0], own_rows, load_sem.at[0])
-    load_rows.start()
 
     @pl.when(works)
     def _():
@@ -72,6 +72,7 @@
             ).start()
 
     pass_on(0)
+    load_rows.start()
     load_rows.wait()
     rows = own_rows[...].astype(jnp.float32)
     lane = lax.broadcasted_iota(jnp.int32, (tok_rows, 128), 1)
@@ -101,28 +102,46 @@
             jnp.where(flag_lane == flag_row // tok_rows, flags[...].astype(jnp.float32), 0.0), axis=-1, keepdims=True
         ) > 0.5
 
-        def prepare(h, state, inverse, number):
-            here = slice(h * head, (h + 1) * head)
-            modded = state * inverse * (1.0 + mod[1, number:number + 1, here]) + mod[0, number:number + 1, here]
-            normed = modded * lax.rsqrt(jnp.mean(modded * modded, axis=-1, keepdims=True) + epsilon)
-            query = (normed * (qg[number:number + 1] * (1.0 / math.sqrt(head)))).astype(jnp.bfloat16)
-            cached_k = cache_k[number, :, here].astype(jnp.float32)
-            cached_v = cache_v[number, :, here].astype(jnp.float32)
-            all_keys = jnp.where(fresh, normed * kg[number:number + 1], cached_k).astype(jnp.bfloat16)
-            all_values = jnp.where(fresh, modded, cached_v).astype(jnp.bfloat16)
-            return query, all_keys, all_values
-
-        def attend(h, state, number, query, all_keys, all_values):
-            here = slice(h * head, (h + 1) * head)
-            scores = lax.dot_general(
-                query, all_keys, (((1,), (1,)), ((), ())), preferred_element_type=jnp.float32
-            )
-            raised = jnp.exp(scores - jnp.max(scores, axis=-1, keepdims=True))
-            total = jnp.sum(raised, axis=-1, keepdims=True)
-            weights = (raised * (1.0 / total)).astype(jnp.bfloat16)
-            attended = jnp.dot(weights, all_values, preferred_element_type=jnp.float32)
-            updated = state + mod[2, number:number + 1, here] * attended
-            return jnp.where(count[...] > number, updated, state)
+        def prepare(numbers, states, inverse, number):
+            modded = []
+            for h, state in zip(numbers, states):
+                here = slice(h * head, (h + 1) * head)
+                modded.append(state * inverse * (1.0 + mod[1, number:number + 1, here]) + mod[0, number:number + 1, here])
+            squared = [jnp.mean(rows * rows, axis=-1, keepdims=True) for rows in modded]
+            ready = []
+            for h, rows, square in zip(numbers, modded, squared):
+                here = slice(h * head, (h + 1) * head)
+                normed = rows * lax.rsqrt(square + epsilon)
+                query = (normed * (qg[number:number + 1] * (1.0 / math.sqrt(head)))).astype(jnp.bfloat16)
+                cached_k = cache_k[number, :, here].astype(jnp.float32)
+                cached_v = cache_v[number, :, here].astype(jnp.float32)
+                all_keys = jnp.where(fresh, normed * kg[number:number + 1], cached_k).astype(jnp.bfloat16)
+                all_values = jnp.where(fresh, rows, cached_v).astype(jnp.bfloat16)
+                ready.append((query, all_keys, all_values))
+            return ready
+
+        def attend(numbers, states, number, ready, first, last):
+            scores = [
+                lax.dot_general(
+                    query[first:last], all_keys, (((1,), (1,)), ((), ())), preferred_element_type=jnp.float32
+                )
+                for query, all_keys, _ in ready
+            ]
+            largest = [jnp.max(score, axis=-1, keepdims=True) for score in scores]
+            raised = [jnp.exp(score - most) for score, most in zip(scores, largest)]
+            scale = [1.0 / jnp.sum(terms, axis=-1, keepdims=True) for terms in raised]
+            weights = [(terms * one).astype(jnp.bfloat16) for terms, one in zip(raised, scale)]
+            attended = [
+                jnp.dot(weight, all_values, preferred_element_type=jnp.float32)
+                for weight, (_, _, all_values) in zip(weights, ready)
+            ]
+            runs = count[...] > number
+            updated = []
+            for h, state, change in zip(numbers, states, attended):
+                rows = state[first:last]
+                moved = rows + mod[2, number:number + 1, h * head:(h + 1) * head] * change
+                updated.append(jnp.where(runs, moved, rows))
+            return updated
 
         pltpu.make_async_copy(inv_in, inv_in, recv_sem.at[0]).wait()
         spread = jnp.broadcast_to(inv_in[...], (patches, tok_rows, 128))
@@ -132,9 +151,9 @@
         for piece in range(PIECES):
             arrived = state_in.at[:, pl.ds(piece * share, share)]
             pltpu.make_async_copy(arrived, arrived, recv_sem.at[4 + piece]).wait()
-            for h in range(piece * heads // PIECES, (piece + 1) * heads // PIECES):
-                state = state_in[:, h * head:(h + 1) * head].astype(jnp.float32)
-                middle.append(attend(h, state, 0, *prepare(h, state, inverse, 0)))
+            numbers = range(piece * heads // PIECES, (piece + 1) * heads // PIECES)
+            states = [state_in[:, h * head:(h + 1) * head].astype(jnp.float32) for h in numbers]
+            middle += attend(numbers, states, 0, prepare(numbers, states, inverse, 0), 0, tokens)
 
         halves = tokens // 128
         lanes = lax.broadcasted_iota(jnp.int32, (128, 128), 1)
@@ -150,10 +169,9 @@
         sums_in[slot] = own_sums[...]
         others = sums_in.at[pl.ds(0, WORKERS - 1)]
         pltpu.make_async_copy(others, others, recv_sem.at[2]).wait()
-        total = jnp.sum(sums_in[...], axis=0)
+        total = lax.rsqrt(jnp.sum(sums_in[...], axis=0) * (1.0 / width) + epsilon)
         spread = jnp.broadcast_to(total[:, None, :], (halves, 128, 128))
-        total = jnp.sum(jnp.where(diagonal, spread, 0.0), axis=-1, keepdims=True).reshape(tokens, 1)
-        inverse = lax.rsqrt(total * (1.0 / width) + epsilon)
+        inverse = jnp.sum(jnp.where(diagonal, spread, 0.0), axis=-1, keepdims=True).reshape(tokens, 1)
 
         pl.semaphore_wait(ready_sem, patches - WORKERS)
 
@@ -177,16 +195,12 @@
             else:
                 send()
 
-        ready = [prepare(h, middle[h], inverse, 1) for h in range(heads)]
-        for first, last in ((0, tokens // 2), (tokens // 2, tokens)):
-            for h in range(heads):
-                query, all_keys, all_values = ready[h]
-                state = attend(h, middle[h][first:last], 1, query[first:last], all_keys, all_values)
+        numbers = range(heads)
+        ready = prepare(numbers, middle, inverse, 1)
+        for first, last, order in STEPS:
+            for h, state in zip(numbers, attend(numbers, middle, 1, ready, first, last)):
                 result[first:last, h * head:(h + 1) * head] = state.astype(result.dtype)
-                if first == 0:
-                    for partner in range(FIRST):
-                        give(partner, h, h + 1)
-            for partner in range(max(first // tok_rows, FIRST), last // tok_rows):
+            for partner in order:
                 give(partner, 0, heads)
         pltpu.make_async_copy(result.at[rows_here, :], out.at[:, column], load_sem.at[8]).wait()
         pltpu.make_async_copy(others, others, send_sem.at[2]).wait()

time: 31.2 us -> 30.2 us (0.968)
  Pallas kernels: 29.7 us -> 28.7 us
    pallas_call x1, Pallas kernels: 29.7 us -> 28.7 us  [per_device(): pl.pallas_call(functools.partial(kernel, sections, patches, head), out_sh...]
where the time goes in v3:
time: 30.2 us; the launch traced here: 30.1 us
  Pallas kernels  28.7 us (95%)
  other arithmetic  0.67 us (2%)
  between operations  0.66 us (2%)
    pallas_call x1, Pallas kernels, per_device(): pl.pallas_call(functools.partial(kernel, sections, patches, head), out_sh...  28.7 us
    broadcast_in_dim x1, other arithmetic, per_device(): return mixed.astype(jnp.float32)[None]  0.67 us

profile of v3, /device:TPU:1, one launch (start us, length us, event | category | flops | bytes accessed | tf_op | source)
XLA Modules:
  0.0 30.1 jit_solution(6988377755439819513)
XLA Ops:
  0.7 28.7 %shard_map.82 = bf16[16,2048]{1,0:T(8,128)(2,1)S(1)} custom-call(bf16[1,16,2048]{2,1,0:T(8,128)(2,1)} %previous.1, bf16[1,2,256,2048]{3,2,1,0:T(8,128)(2,1)} %stale_k.1, bf16[1,2,256,2048]{3,2,1,0:T(8,128)(2,1)} %stale_v.1, f32[1,3,2,2048]{3,2,1,0:T(2,128)} %bitcast.6, f32[1,2,128]{2,1,0:T(2,128)} %q_gain.1, f32[1,2,128]{2,1,0:T(2,128)} %k_gain.1, ...), custom_call_target="tpu_custom_call" | custom-call | tf_op jit(solution)/shard_map/pallas_call | solution.py:231
  29.4 0.7 %bitcast_convert_fusion = f32[1,16,2048]{2,1,0:T(8,128)} fusion(bf16[16,2048]{1,0:T(8,128)(2,1)S(1)} %shard_map.82), kind=kLoop, calls=%fused_computation | loop fusion | flops 32768 | bytes 196608 | tf_op jit(solution)/shard_map/broadcast_in_dim | solution.py:260

commit v4 on v3

--- a/solution.py
+++ b/solution.py
@@ -63,10 +63,13 @@
 
     pl.semaphore_wait(barrier, 2 * WORKERS - works.astype(jnp.int32))
 
+    order = range(WORKERS - 1, -1, -1)
+
     def pass_on(piece):
-        for index in range(WORKERS):
+        for index in order:
+            begin = pl.multiple_of(index * part + piece * share, share)
             pltpu.make_async_remote_copy(
-                src_ref=previous.at[0, :, pl.ds(index * part + piece * share, share)],
+                src_ref=previous.at[0, :, pl.ds(begin, share)],
                 dst_ref=state_in.at[rows_here, pl.ds(piece * share, share)],
                 send_sem=send_sem.at[1], recv_sem=recv_sem.at[4 + piece], **to(after, FIRST + index),
             ).start()
@@ -79,7 +82,7 @@
     row = lax.broadcasted_iota(jnp.int32, (tok_rows, 128), 0)
     inverse = lax.rsqrt(jnp.mean(rows * rows, axis=-1, keepdims=True) + epsilon)
     own_inv[...] = jnp.sum(jnp.where(lane == row, inverse, 0.0), axis=0, keepdims=True)
-    for index in range(WORKERS):
+    for index in order:
         pltpu.make_async_remote_copy(
             src_ref=own_inv, dst_ref=inv_in.at[patch],
             send_sem=send_sem.at[0], recv_sem=recv_sem.at[0], **to(after, FIRST + index),

time: 30.2 us -> 30 us (level)
  no operation moved by 1% of the time
where the time goes in v4:
time: 30 us; the launch traced here: 29.8 us
  Pallas kernels  28.5 us (95%)
  other arithmetic  0.67 us (2%)
  between operations  0.66 us (2%)
    pallas_call x1, Pallas kernels, per_device(): pl.pallas_call(functools.partial(kernel, sections, patches, head), out_sh...  28.5 us
    broadcast_in_dim x1, other arithmetic, per_device(): return mixed.astype(jnp.float32)[None]  0.67 us

profile of v4, /device:TPU:1, one launch (start us, length us, event | category | flops | bytes accessed | tf_op | source)
XLA Modules:
  0.0 29.8 jit_solution(7478988410095778786)
XLA Ops:
  0.7 28.5 %shard_map.82 = bf16[16,2048]{1,0:T(8,128)(2,1)S(1)} custom-call(bf16[1,16,2048]{2,1,0:T(8,128)(2,1)} %previous.1, bf16[1,2,256,2048]{3,2,1,0:T(8,128)(2,1)} %stale_k.1, bf16[1,2,256,2048]{3,2,1,0:T(8,128)(2,1)} %stale_v.1, f32[1,3,2,2048]{3,2,1,0:T(2,128)} %bitcast.6, f32[1,2,128]{2,1,0:T(2,128)} %q_gain.1, f32[1,2,128]{2,1,0:T(2,128)} %k_gain.1, ...), custom_call_target="tpu_custom_call" | custom-call | tf_op jit(solution)/shard_map/pallas_call | solution.py:234
  29.1 0.7 %bitcast_convert_fusion = f32[1,16,2048]{2,1,0:T(8,128)} fusion(bf16[16,2048]{1,0:T(8,128)(2,1)S(1)} %shard_map.82), kind=kLoop, calls=%fused_computation | loop fusion | flops 32768 | bytes 196608 | tf_op jit(solution)/shard_map/broadcast_in_dim | solution.py:263

commit v5 on v4

--- a/solution.py
+++ b/solution.py
@@ -12,7 +12,7 @@
 VMEM_BYTES = 48 * 2**20
 MESH = pl.DeviceIdType.MESH
 PIECES = 2
-STEPS = ((0, 256, (1, 3, 2, 0, 4, 5, 6, 7, 14, 15, 8, 9, 12, 13, 10, 11)),)
+STEPS = ((0, 128, (1, 3, 2, 0, 4, 5, 6, 7)), (128, 256, (14, 15, 8, 9, 12, 13, 10, 11)))
 FIRST, WORKERS = 2, 4
 
 
@@ -103,7 +103,8 @@
             load.wait()
         fresh = jnp.sum(
             jnp.where(flag_lane == flag_row // tok_rows, flags[...].astype(jnp.float32), 0.0), axis=-1, keepdims=True
-        ) > 0.5
+        )
+        fresh = jnp.broadcast_to(fresh, (tokens, head)).astype(jnp.bfloat16) > 0.5
 
         def prepare(numbers, states, inverse, number):
             modded = []
@@ -116,10 +117,9 @@
                 here = slice(h * head, (h + 1) * head)
                 normed = rows * lax.rsqrt(square + epsilon)
                 query = (normed * (qg[number:number + 1] * (1.0 / math.sqrt(head)))).astype(jnp.bfloat16)
-                cached_k = cache_k[number, :, here].astype(jnp.float32)
-                cached_v = cache_v[number, :, here].astype(jnp.float32)
-                all_keys = jnp.where(fresh, normed * kg[number:number + 1], cached_k).astype(jnp.bfloat16)
-                all_values = jnp.where(fresh, rows, cached_v).astype(jnp.bfloat16)
+                fresh_k = (normed * kg[number:number + 1]).astype(jnp.bfloat16)
+                all_keys = jnp.where(fresh, fresh_k, cache_k[number, :, here])
+                all_values = jnp.where(fresh, rows.astype(jnp.bfloat16), cache_v[number, :, here])
                 ready.append((query, all_keys, all_values))
             return ready
 
@@ -154,9 +154,8 @@
         for piece in range(PIECES):
             arrived = state_in.at[:, pl.ds(piece * share, share)]
             pltpu.make_async_copy(arrived, arrived, recv_sem.at[4 + piece]).wait()
-            numbers = range(piece * heads // PIECES, (piece + 1) * heads // PIECES)
-            states = [state_in[:, h * head:(h + 1) * head].astype(jnp.float32) for h in numbers]
-            middle += attend(numbers, states, 0, prepare(numbers, states, inverse, 0), 0, tokens)
+        states = [state_in[:, h * head:(h + 1) * head].astype(jnp.float32) for h in range(heads)]
+        middle = attend(range(heads), states, 0, prepare(range(heads), states, inverse, 0), 0, tokens)
 
         halves = tokens // 128
         lanes = lax.broadcasted_iota(jnp.int32, (128, 128), 1)

time: 30 us -> 29.7 us (0.990)
  Pallas kernels: 28.5 us -> 28.2 us
where the time goes in v5:
time: 29.7 us; the launch traced here: 29.6 us
  Pallas kernels  28.2 us (95%)
  other arithmetic  0.67 us (2%)
  between operations  0.66 us (2%)
    pallas_call x1, Pallas kernels, per_device(): pl.pallas_call(functools.partial(kernel, sections, patches, head), out_sh...  28.2 us
    broadcast_in_dim x1, other arithmetic, per_device(): return mixed.astype(jnp.float32)[None]  0.67 us

profile of v5, /device:TPU:1, one launch (start us, length us, event | category | flops | bytes accessed | tf_op | source)
XLA Modules:
  0.0 29.6 jit_solution(2936595687490539999)
XLA Ops:
  0.7 28.2 %shard_map.82 = bf16[16,2048]{1,0:T(8,128)(2,1)S(1)} custom-call(bf16[1,16,2048]{2,1,0:T(8,128)(2,1)} %previous.1, bf16[1,2,256,2048]{3,2,1,0:T(8,128)(2,1)} %stale_k.1, bf16[1,2,256,2048]{3,2,1,0:T(8,128)(2,1)} %stale_v.1, f32[1,3,2,2048]{3,2,1,0:T(2,128)} %bitcast.6, f32[1,2,128]{2,1,0:T(2,128)} %q_gain.1, f32[1,2,128]{2,1,0:T(2,128)} %k_gain.1, ...), custom_call_target="tpu_custom_call" | custom-call | tf_op jit(solution)/shard_map/pallas_call | solution.py:233
  28.9 0.7 %bitcast_convert_fusion = f32[1,16,2048]{2,1,0:T(8,128)} fusion(bf16[16,2048]{1,0:T(8,128)(2,1)S(1)} %shard_map.82), kind=kLoop, calls=%fused_computation | loop fusion | flops 32768 | bytes 196608 | tf_op jit(solution)/shard_map/broadcast_in_dim | solution.py:262

commit v6 on v5

--- a/solution.py
+++ b/solution.py
@@ -54,14 +54,10 @@
     def _():
         for partner in range(patches - 1, -1, -1):
             pl.semaphore_signal(barrier, inc=1, **to(before, partner))
-        for partner in range(patches - 1, -1, -1):
-            @pl.when(partner != patch)
-            def _():
-                pl.semaphore_signal(barrier, inc=1, **to(section, partner))
         for load in loads:
             load.start()
 
-    pl.semaphore_wait(barrier, 2 * WORKERS - works.astype(jnp.int32))
+    pl.semaphore_wait(barrier, WORKERS)
 
     order = range(WORKERS - 1, -1, -1)
 
@@ -89,11 +85,6 @@
         ).start()
     for piece in range(1, PIECES):
         pass_on(piece)
-
-    @pl.when(jnp.logical_not(works))
-    def _():
-        for index in range(WORKERS):
-            pl.semaphore_signal(ready_sem, inc=1, **to(section, FIRST + index))
 
     @pl.when(works)
     def _():
@@ -154,6 +145,7 @@
         for piece in range(PIECES):
             arrived = state_in.at[:, pl.ds(piece * share, share)]
             pltpu.make_async_copy(arrived, arrived, recv_sem.at[4 + piece]).wait()
+        pl.semaphore_signal(ready_sem, inc=1, **to(before, patch))
         states = [state_in[:, h * head:(h + 1) * head].astype(jnp.float32) for h in range(heads)]
         middle = attend(range(heads), states, 0, prepare(range(heads), states, inverse, 0), 0, tokens)
 
@@ -175,7 +167,7 @@
         spread = jnp.broadcast_to(total[:, None, :], (halves, 128, 128))
         inverse = jnp.sum(jnp.where(diagonal, spread, 0.0), axis=-1, keepdims=True).reshape(tokens, 1)
 
-        pl.semaphore_wait(ready_sem, patches - WORKERS)
+        pl.semaphore_wait(ready_sem, 1)
 
         def give(partner, first, last):
             rows_there = pl.ds(partner * tok_rows, tok_rows)

time: 29.7 us -> 29.7 us (level)
  no operation moved by 1% of the time
where the time goes in v6:
time: 29.7 us; the launch traced here: 29.6 us
  Pallas kernels  28.2 us (95%)
  other arithmetic  0.67 us (2%)
  between operations  0.66 us (2%)
    pallas_call x1, Pallas kernels, per_device(): pl.pallas_call(functools.partial(kernel, sections, patches, head), out_sh...  28.2 us
    broadcast_in_dim x1, other arithmetic, per_device(): return mixed.astype(jnp.float32)[None]  0.67 us

profile of v6, /device:TPU:1, one launch (start us, length us, event | category | flops | bytes accessed | tf_op | source)
XLA Modules:
  0.0 29.6 jit_solution(2552049657369380953)
XLA Ops:
  0.7 28.2 %shard_map.82 = bf16[16,2048]{1,0:T(8,128)(2,1)S(1)} custom-call(bf16[1,16,2048]{2,1,0:T(8,128)(2,1)} %previous.1, bf16[1,2,256,2048]{3,2,1,0:T(8,128)(2,1)} %stale_k.1, bf16[1,2,256,2048]{3,2,1,0:T(8,128)(2,1)} %stale_v.1, f32[1,3,2,2048]{3,2,1,0:T(2,128)} %bitcast.6, f32[1,2,128]{2,1,0:T(2,128)} %q_gain.1, f32[1,2,128]{2,1,0:T(2,128)} %k_gain.1, ...), custom_call_target="tpu_custom_call" | custom-call | tf_op jit(solution)/shard_map/pallas_call | solution.py:225
  28.9 0.7 %bitcast_convert_fusion = f32[1,16,2048]{2,1,0:T(8,128)} fusion(bf16[16,2048]{1,0:T(8,128)(2,1)S(1)} %shard_map.82), kind=kLoop, calls=%fused_computation | loop fusion | flops 32768 | bytes 196608 | tf_op jit(solution)/shard_map/broadcast_in_dim | solution.py:254

commit v7 on v5

--- a/solution.py
+++ b/solution.py
@@ -28,6 +28,7 @@
     tok_rows, width = own_rows.shape
     tokens, part = state_in.shape
     share = part // PIECES
+    layers = cache_k.shape[0]
     works = jnp.logical_and(patch >= FIRST, patch < FIRST + WORKERS)
     slot = lax.rem(patch + patches - FIRST, patches)
     mine = lax.rem(slot, WORKERS)
@@ -132,12 +133,26 @@
             ]
             largest = [jnp.max(score, axis=-1, keepdims=True) for score in scores]
             raised = [jnp.exp(score - most) for score, most in zip(scores, largest)]
+            if number == layers - 1:
+                product = [
+                    jnp.dot(
+                        terms.astype(jnp.bfloat16),
+                        jnp.concatenate([all_values, jnp.ones_like(all_values)], axis=1),
+                        preferred_element_type=jnp.float32,
+                    )
+                    for terms, (_, _, all_values) in zip(raised, ready)
+                ]
+                attended = [both[:, :head] / both[:, head:] for both in product]
+                return settle(numbers, states, number, attended, first, last)
             scale = [1.0 / jnp.sum(terms, axis=-1, keepdims=True) for terms in raised]
             weights = [(terms * one).astype(jnp.bfloat16) for terms, one in zip(raised, scale)]
             attended = [
                 jnp.dot(weight, all_values, preferred_element_type=jnp.float32)
                 for weight, (_, _, all_values) in zip(weights, ready)
             ]
+            return settle(numbers, states, number, attended, first, last)
+
+        def settle(numbers, states, number, attended, first, last):
             runs = count[...] > number
             updated = []
             for h, state, change in zip(numbers, states, attended):

time: 29.7 us -> 29.6 us (level)
  no operation moved by 1% of the time
where the time goes in v7:
time: 29.6 us; the launch traced here: 29.5 us
  Pallas kernels  28.2 us (95%)
  other arithmetic  0.67 us (2%)
  between operations  0.66 us (2%)
    pallas_call x1, Pallas kernels, per_device(): pl.pallas_call(functools.partial(kernel, sections, patches, head), out_sh...  28.2 us
    broadcast_in_dim x1, other arithmetic, per_device(): return mixed.astype(jnp.float32)[None]  0.67 us

profile of v7, /device:TPU:1, one launch (start us, length us, event | category | flops | bytes accessed | tf_op | source)
XLA Modules:
  0.0 29.5 jit_solution(15368945651134032479)
XLA Ops:
  0.7 28.2 %shard_map.82 = bf16[16,2048]{1,0:T(8,128)(2,1)S(1)} custom-call(bf16[1,16,2048]{2,1,0:T(8,128)(2,1)} %previous.1, bf16[1,2,256,2048]{3,2,1,0:T(8,128)(2,1)} %stale_k.1, bf16[1,2,256,2048]{3,2,1,0:T(8,128)(2,1)} %stale_v.1, f32[1,3,2,2048]{3,2,1,0:T(2,128)} %bitcast.6, f32[1,2,128]{2,1,0:T(2,128)} %q_gain.1, f32[1,2,128]{2,1,0:T(2,128)} %k_gain.1, ...), custom_call_target="tpu_custom_call" | custom-call | tf_op jit(solution)/shard_map/pallas_call | solution.py:248
  28.8 0.7 %bitcast_convert_fusion = f32[1,16,2048]{2,1,0:T(8,128)} fusion(bf16[16,2048]{1,0:T(8,128)(2,1)S(1)} %shard_map.82), kind=kLoop, calls=%fused_computation | loop fusion | flops 32768 | bytes 196608 | tf_op jit(solution)/shard_map/broadcast_in_dim | solution.py:277
